TPU v7x, 512 devices: a whole 4x4x16 slice. The times are simulated.
512 devices in a mesh: ctx: 128 (over z, x, core), grp: 4 (over y).
Axes of the slice: x: 4, y: 4, z: 16, core: 2. Of those that a mesh axis runs over, the one named last changes fastest.
Arguments:
- queries: bfloat16 [16384, 12288], P('ctx', 'grp'), parts along dimension 1, may hold values from -250 to 250
- keys: bfloat16 [2, 16384, 768], P(None, 'ctx', 'grp'), parts along dimension 2, may hold values from -6 to 6
- values: bfloat16 [2, 16384, 512], P(None, 'ctx', 'grp'), parts along dimension 2, may hold values from -6 to 6
- gate_logits: bfloat16 [16384, 192], P('ctx', 'grp'), parts along dimension 1, may hold values from -6 to 6
- sel_ids: int32 [1024, 64], P('ctx', 'grp'), parts along dimension 1, may hold values from -1 to 511, as said below
- pos_k: bfloat16 [32, 768], P(None, 'grp'), parts along dimension 1, may hold values from -1 to 1
- pos_v: bfloat16 [32, 512], P(None, 'grp'), parts along dimension 1, may hold values from -1 to 1
- mix_k: bfloat16 [192, 768], P(None, 'grp'), parts along dimension 1, may hold values from -0.4375 to 0.4375
- mix_v: bfloat16 [128, 512], P(None, 'grp'), parts along dimension 1, may hold values from -0.5 to 0.5
Outputs:
- attended: bfloat16 [16384, 8192], P('ctx', 'grp'), parts along dimension 1
There are 4 independent parts, one for each index of `grp`. A program takes and returns all parts, laid end to end along the dimension named above; each array names one. Nothing has to cross between parts.
Inputs may be any that keep to these rules, and one draw needn't show every extreme that they name: `sel_ids`: the first entry of a row is the block that holds the row's tokens. The other entries name distinct blocks that lie wholly before position 16384, or are -1 at the row's end; each row has at least 12 entries that are not -1. Over the 8 rows of one device, the entries after the first name at most 64 = min(64, 1 * 2 * 128) distinct blocks, at most 1 of them held by one device, and no block in more than 2 rows.
All inputs are finite; a program needn't handle non-finite values.
Results may differ from a plain program's by a relative error of at most 0.011.
Values may be sent and summed in bfloat16 or wider, within the bound.
A program may use at most 128 MiB of HBM per device.

v0:
```python
import jax
import jax.numpy as jnp
from jax import lax
from jax.sharding import PartitionSpec as P

HEADS = 16
DK = 192
DV = 128
CMP_BLOCK = 32
SEL_BLOCK = 64
QBLOCK = 16
SPREAD = 64


def shifted(value, axis, steps):
    count = lax.axis_size(axis)
    pairs = [(source, (source + steps) % count) for source in range(count)]
    return lax.ppermute(value, axis, pairs)


def sent_together(arrays, axis, dim, along):
    ends, at = ([], 0)
    for a in arrays[:-1]:
        at += a.shape[along]
        ends.append(at)
    both = jnp.concatenate(arrays, axis=along)
    return tuple(jnp.split(lax.all_gather(both, axis, axis=dim, tiled=True), ends, axis=along))


def attention(query_rows, key_rows, value_rows, allowed, head_count):
    scores = jnp.dot(query_rows, key_rows.T, preferred_element_type=jnp.float32) * query_rows.shape[
        1
    ] ** (-0.5)
    scores = scores.reshape(-1, head_count, key_rows.shape[0])
    scores = jnp.where(allowed[:, None, :], scores, -jnp.inf)
    highest = jnp.max(scores, axis=2, keepdims=True)
    weights = jnp.exp(scores - highest)
    totals = jnp.sum(weights, axis=2)
    rounded = weights.astype(jnp.bfloat16).reshape(-1, key_rows.shape[0])
    mixture = jnp.dot(rounded, value_rows, preferred_element_type=jnp.float32)
    return mixture.reshape(-1, head_count, value_rows.shape[1]) / totals[:, :, None]


def body(queries, keys, values, gate_logits, sel_ids, pos_k, pos_v, mix_k, mix_v):
    devices = lax.axis_size("ctx")
    myself = lax.axis_index("ctx")
    rounds = keys.shape[0]
    cached = rounds - 1
    tokens = keys.shape[1]
    scaling = DK ** (-0.5)
    query_rows = queries.reshape(tokens * HEADS, DK)
    query_pos = (cached * devices + myself) * tokens + jnp.arange(tokens, dtype=jnp.int32)
    paired = jnp.concatenate([keys, values], axis=2)
    earlier_rows = []
    for shift_by in range(1, 5):
        wrapped = myself + shift_by >= devices
        outgoing = jnp.where(wrapped, paired[0], paired[1])
        earlier_rows.append(shifted(outgoing, "ctx", shift_by))
    per_piece = tokens // CMP_BLOCK
    local_count = rounds * per_piece
    pooled_k = jnp.einsum(
        "bjd,jd->bd",
        keys.reshape(local_count, CMP_BLOCK, DK),
        pos_k,
        preferred_element_type=jnp.float32,
    ).astype(jnp.bfloat16)
    pooled_v = jnp.einsum(
        "bjd,jd->bd",
        values.reshape(local_count, CMP_BLOCK, DV),
        pos_v,
        preferred_element_type=jnp.float32,
    ).astype(jnp.bfloat16)
    comp_keys = jnp.dot(pooled_k, mix_k, preferred_element_type=jnp.float32).astype(jnp.bfloat16)
    comp_values = jnp.dot(pooled_v, mix_v, preferred_element_type=jnp.float32).astype(jnp.bfloat16)
    all_keys, all_values = sent_together((comp_keys, comp_values), "ctx", 0, 1)
    length = all_keys.shape[0]
    summed = jnp.zeros((tokens, HEADS, DV), jnp.float32)
    highest = jnp.full((tokens, HEADS), -jnp.inf, jnp.float32)
    totals = jnp.zeros((tokens, HEADS), jnp.float32)
    for low_row in range(0, length, 512):
        high_row = min(length, low_row + 512)
        key_index = low_row + jnp.arange(high_row - low_row, dtype=jnp.int32)
        holder = key_index // local_count
        within = key_index % local_count
        end_pos = (
            (within // per_piece * devices + holder) * tokens
            + (within % per_piece + 1) * CMP_BLOCK
            - 1
        )
        allowed = end_pos[None, :] <= query_pos[:, None]
        scores = (
            jnp.dot(query_rows, all_keys[low_row:high_row].T, preferred_element_type=jnp.float32)
            * scaling
        )
        scores = jnp.where(
            allowed[:, None, :], scores.reshape(tokens, HEADS, high_row - low_row), -jnp.inf
        )
        raised = jnp.maximum(highest, jnp.max(scores, axis=2))
        anchor = jnp.where(raised == -jnp.inf, 0.0, raised)
        weights = jnp.exp(scores - anchor[:, :, None])
        factor = jnp.exp(highest - anchor)
        totals = totals * factor + jnp.sum(weights, axis=2)
        mixture = jnp.dot(
            weights.astype(jnp.bfloat16).reshape(tokens * HEADS, high_row - low_row),
            all_values[low_row:high_row],
            preferred_element_type=jnp.float32,
        )
        summed = summed * factor[:, :, None] + mixture.reshape(tokens, HEADS, DV)
        highest = raised
    compressed = summed / totals[:, :, None]
    window_rows = jnp.concatenate(earlier_rows[::-1] + [paired[1]], axis=0)
    column = jnp.arange(5 * tokens, dtype=jnp.int32)[None, :]
    offsets = jnp.arange(tokens, dtype=jnp.int32)[:, None]
    inside = (column > offsets) & (column <= 4 * tokens + offsets)
    sliding = attention(query_rows, window_rows[:, :DK], window_rows[:, DK:], inside, HEADS)
    per_block = tokens // SEL_BLOCK
    groups = sel_ids.shape[0]
    listed = sel_ids.shape[1]
    remote = sel_ids[:, 1:].reshape(-1)
    entries = remote.shape[0]
    usable = remote >= 0
    clipped = jnp.maximum(remote, 0)
    holder_piece = clipped // per_block
    holder = holder_piece % devices
    local_block = holder_piece // devices * per_block + clipped % per_block
    distinct = min(SPREAD, cached * per_block * devices)
    per_owner = -(-distinct // devices)
    earlier = jnp.arange(entries)[None, :] < jnp.arange(entries)[:, None]
    same_owner = holder[:, None] == holder[None, :]
    key_blocks = keys.reshape(rounds * per_block, SEL_BLOCK, DK)
    value_blocks = values.reshape(rounds * per_block, SEL_BLOCK, DV)
    repeated = (remote[:, None] == remote[None, :]) & usable[None, :] & earlier
    leading = usable & ~jnp.any(repeated, axis=1)
    before = same_owner & leading[None, :] & earlier
    slot_of = holder * per_owner + jnp.sum(before, axis=1)
    first_seen = jnp.argmax(repeated, axis=1)
    fetch_at = jnp.where(leading, slot_of, slot_of[first_seen])
    target = jnp.where(leading, slot_of, devices * per_owner)
    requests = (
        jnp.full((devices * per_owner,), -1, jnp.int32).at[target].set(local_block, mode="drop")
    )
    wanted = lax.all_to_all(
        requests.reshape(devices, per_owner), "ctx", split_axis=0, concat_axis=0, tiled=True
    )
    chosen = jnp.maximum(wanted, 0)
    out_keys = key_blocks[chosen].reshape(devices, per_owner, SEL_BLOCK * DK)
    out_values = value_blocks[chosen].reshape(devices, per_owner, SEL_BLOCK * DV)
    got_keys, got_values = (
        lax.all_to_all(out_keys, "ctx", split_axis=0, concat_axis=0, tiled=True),
        lax.all_to_all(out_values, "ctx", split_axis=0, concat_axis=0, tiled=True),
    )
    near_keys = got_keys.reshape(devices * per_owner, SEL_BLOCK, DK)[fetch_at]
    near_values = got_values.reshape(devices * per_owner, SEL_BLOCK, DV)[fetch_at]
    own_index = cached * per_block + jnp.arange(groups, dtype=jnp.int32) * QBLOCK // SEL_BLOCK
    block_keys = jnp.concatenate(
        [key_blocks[own_index][:, None], near_keys.reshape(groups, listed - 1, SEL_BLOCK, DK)],
        axis=1,
    )
    block_values = jnp.concatenate(
        [value_blocks[own_index][:, None], near_values.reshape(groups, listed - 1, SEL_BLOCK, DV)],
        axis=1,
    )
    key_count = listed * SEL_BLOCK
    block_keys = block_keys.reshape(groups, key_count, DK)
    block_values = block_values.reshape(groups, key_count, DV)
    own_pos = (own_index - cached * per_block)[:, None] * SEL_BLOCK + jnp.arange(
        SEL_BLOCK, dtype=jnp.int32
    )[None, :]
    query_off = (
        jnp.arange(groups, dtype=jnp.int32)[:, None] * QBLOCK
        + jnp.arange(QBLOCK, dtype=jnp.int32)[None, :]
    )
    own_allowed = own_pos[:, None, :] <= query_off[:, :, None]
    far_allowed = jnp.repeat(usable.reshape(groups, listed - 1), SEL_BLOCK, axis=1)
    allowed = jnp.concatenate(
        [
            own_allowed,
            jnp.broadcast_to(far_allowed[:, None, :], (groups, QBLOCK, (listed - 1) * SEL_BLOCK)),
        ],
        axis=2,
    )
    grouped_q = queries.reshape(groups, QBLOCK * HEADS, DK)
    scores = (
        jnp.einsum("aqd,akd->aqk", grouped_q, block_keys, preferred_element_type=jnp.float32)
        * scaling
    )
    scores = jnp.where(
        allowed[:, :, None, :], scores.reshape(groups, QBLOCK, HEADS, key_count), -jnp.inf
    )
    sel_highest = jnp.max(scores, axis=3, keepdims=True)
    weights = jnp.exp(scores - sel_highest)
    sel_totals = jnp.sum(weights, axis=3)
    mixture = jnp.einsum(
        "aqk,akd->aqd",
        weights.astype(jnp.bfloat16).reshape(groups, QBLOCK * HEADS, key_count),
        block_values,
        preferred_element_type=jnp.float32,
    )
    selected = mixture.reshape(tokens, HEADS, DV) / sel_totals.reshape(tokens, HEADS)[:, :, None]
    gate_values = jax.nn.sigmoid(gate_logits.astype(jnp.float32)).reshape(tokens, 3, HEADS)
    combined = (
        gate_values[:, 0, :, None] * compressed
        + gate_values[:, 1, :, None] * selected
        + gate_values[:, 2, :, None] * sliding
    )
    return combined.reshape(tokens, HEADS * DV).astype(jnp.bfloat16)


def solution(mesh):
    in_specs = (
        P("ctx", "grp"),
        P(None, "ctx", "grp"),
        P(None, "ctx", "grp"),
        P("ctx", "grp"),
        P("ctx", "grp"),
        P(None, "grp"),
        P(None, "grp"),
        P(None, "grp"),
        P(None, "grp"),
    )
    out_specs = P("ctx", "grp")
    return jax.shard_map(body, mesh=mesh, in_specs=in_specs, out_specs=out_specs, check_vma=False)
```

profile of v0, /device:TPU:1, one launch (start us, length us, event | category | flops | bytes accessed | tf_op | source)
XLA Modules:
  0.0 559.6 jit_solution(16905903628946677655)
XLA Ops:
  5.4 35.1 %all_to_all.19 = s32[128,1,1]{2,1,0:T(1,128)S(1)} all-to-all(s32[128,1,1]{2,1,0:T(1,128)S(1)} %copy.189), channel_id=1, replica_groups=mesh['ctx'=128,'grp'=4] {'ctx'}, dimensions={0} | all-to-all | bytes 1024 | tf_op jit(solution)/shard_map/all_to_all | solution.py:142
  40.5 2.4 maximum_reduce_fusion
  43.5 3.0 gather_fusion.5
  46.5 3.3 copy.198
  50.3 2.9 reduce.33
  53.2 2.9 copy.257
  56.1 2.8 reshape.784
  58.9 6.1 %all-to-all-start.2 = ((bf16[128,2,4096]{2,1,0:T(2,128)(2,1)}), bf16[128,2,4096]{2,1,0:T(2,128)(2,1)S(1)}, u32[]{:S(2)}, u32[]{:S(2)}) async-start(bf16[128,2,4096]{2,1,0:T(2,128)(2,1)} %reshape.784), calls=%async_computation.2 | async-start | bytes 4194304 | tf_op jit(solution)/shard_map/all_to_all | solution.py:150
  65.2 2.7 gather_fusion.1
  67.9 6.7 %copy.190 = bf16[128,64,192]{0,2,1:T(8,128)(2,1)} copy(bf16[128,64,192]{2,1,0:T(8,128)(2,1)} %gather_fusion.1) | data formatting | bytes 6291456 | tf_op jit(solution)/shard_map/gather | solution.py:146
  74.6 5.3 reduce.34
  79.9 4.7 copy.258
  84.6 8.0 %reshape.786 = bf16[128,2,6144]{2,1,0:T(2,128)(2,1)} reshape(bf16[128,12288]{1,0:T(8,128)(2,1)} %copy.258) | data formatting | bytes 6291456
  92.6 69.2 %all-to-all-done.2 = bf16[128,2,4096]{2,1,0:T(2,128)(2,1)S(1)} async-done(((bf16[128,2,4096]{2,1,0:T(2,128)(2,1)}), bf16[128,2,4096]{2,1,0:T(2,128)(2,1)S(1)}, u32[]{:S(2)}, u32[]{:S(2)}) %all-to-all-start.2) | async-done | bytes 2097184 | tf_op jit(solution)/shard_map/all_to_all | solution.py:150
  161.8 10.6 %all-to-all-start.1 = ((bf16[128,2,6144]{2,1,0:T(2,128)(2,1)}), bf16[128,2,6144]{2,1,0:T(2,128)(2,1)}, u32[]{:S(2)}, u32[]{:S(2)}) async-start(bf16[128,2,6144]{2,1,0:T(2,128)(2,1)} %reshape.786), calls=%async_computation.1 | async-start | bytes 6291456 | tf_op jit(solution)/shard_map/all_to_all | solution.py:149
  173.9 4.8 collective-permute-start
  178.7 3.6 collective-permute-start.1
  182.3 3.1 collective-permute-start.2
  185.4 2.8 collective-permute-start.3
  190.7 2.1 reshape.700
  192.8 2.2 reshape.694
  200.7 205.6 %all_gather.3 = bf16[1024,320]{1,0:T(8,128)(2,1)S(1)} all-gather(bf16[8,320]{1,0:T(8,128)(2,1)S(1)} %pad_maximum_fusion.3), channel_id=1, replica_groups=mesh['ctx'=128,'grp'=4] {'ctx'}, dimensions={0}, use_global_device_ids=true | all-gather | bytes 660480 | tf_op jit(solution)/shard_map/all_gather | solution.py:27
  406.3 2.8 fusion.103
  409.2 3.8 fusion.104
  413.1 4.1 fusion.13
  417.3 2.9 fusion.10
  424.2 2.7 copy.179
  428.1 5.1 fusion.24
  434.1 3.9 copy.197
  438.4 2.5 copy.207
  440.9 3.9 copy.184
  448.6 2.6 fusion.105
  451.2 2.3 fusion.2
  453.5 4.4 copy.208
  457.9 2.7 fusion.46
  462.2 13.9 %reshape.785 = bf16[128,1,8192]{2,1,0:T(2,128)(2,1)} reshape(bf16[128,2,4096]{2,1,0:T(2,128)(2,1)} %copy-done.3) | data formatting | bytes 4194304
  476.0 9.1 %copy.200 = bf16[128,1,8192]{0,2,1:T(8,128)(2,1)} copy(bf16[128,1,8192]{2,1,0:T(2,128)(2,1)} %reshape.785) | data formatting | bytes 4194304 | tf_op jit(solution)/shard_map/all_to_all | solution.py:150
  485.2 4.2 copy.201
  489.4 3.8 gather_fusion.6
  493.2 3.1 pad_maximum_fusion.1
  496.3 19.6 %reshape.787 = bf16[128,1,12288]{2,1,0:T(2,128)(2,1)} reshape(bf16[128,2,6144]{2,1,0:T(2,128)(2,1)} %all-to-all-done.1) | data formatting | bytes 6291456
  515.9 13.3 %copy.192 = bf16[128,1,12288]{0,2,1:T(8,128)(2,1)} copy(bf16[128,1,12288]{2,1,0:T(2,128)(2,1)} %reshape.787) | data formatting | bytes 6291456 | tf_op jit(solution)/shard_map/all_to_all | solution.py:149
  529.2 6.7 %copy.193 = bf16[128,64,192]{2,1,0:T(8,128)(2,1)} copy(bf16[128,64,192]{0,2,1:T(8,128)(2,1)} %bitcast.112) | data formatting | bytes 6291456 | tf_op jit(solution)/shard_map/reshape | solution.py:152
  535.9 5.1 gather_fusion.3
  541.0 2.9 pad_maximum_fusion
  545.8 2.2 fusion
  548.1 3.7 fusion.5
  553.5 4.7 fusion.39
  (116 shorter events, 32.5 us)
Async XLA Ops:
  0.0 200.4 %copy-start = (bf16[192,192]{1,0:T(8,128)(2,1)S(1)}, bf16[192,192]{1,0:T(8,128)(2,1)}, u32[]{:S(2)}) copy-start(bf16[192,192]{1,0:T(8,128)(2,1)} %param.16) | copy-start | bytes 221188
  56.1 9.0 %copy-start.12 = (bf16[2,128,192]{1,2,0:T(8,128)(2,1)S(1)}, bf16[2,128,192]{1,2,0:T(8,128)(2,1)}, u32[]{:S(2)}) copy-start(bf16[2,128,192]{1,2,0:T(8,128)(2,1)} %param.10) | copy-start | bytes 294916
  58.9 102.9 %all-to-all-start.2 = ((bf16[128,2,4096]{2,1,0:T(2,128)(2,1)}), bf16[128,2,4096]{2,1,0:T(2,128)(2,1)S(1)}, u32[]{:S(2)}, u32[]{:S(2)}) async-start(bf16[128,2,4096]{2,1,0:T(2,128)(2,1)} %reshape.784), calls=%async_computation.2 | async-start | bytes 4194304 | tf_op jit(solution)/shard_map/all_to_all | solution.py:150
  92.6 79.8 %copy-start.2 = (bf16[2,128,128]{2,1,0:T(8,128)(2,1)S(1)}, bf16[2,128,128]{2,1,0:T(8,128)(2,1)}, u32[]{:S(2)}) copy-start(bf16[2,128,128]{2,1,0:T(8,128)(2,1)} %param.11) | copy-start | bytes 196612
  92.6 98.1 %copy-start.5 = (bf16[128,3072]{1,0:T(8,128)(2,1)S(1)}, bf16[128,3072]{1,0:T(8,128)(2,1)}, u32[]{:S(2)}) copy-start(bf16[128,3072]{1,0:T(8,128)(2,1)} %param.9) | copy-start | bytes 2359300
  161.8 28.9 %copy-start.3 = (bf16[128,2,4096]{2,1,0:T(2,128)(2,1)}, bf16[128,2,4096]{2,1,0:T(2,128)(2,1)S(1)}, u32[]{:S(2)}) copy-start(bf16[128,2,4096]{2,1,0:T(2,128)(2,1)S(1)} %all-to-all-done.2) | copy-start | bytes 6291460
  161.8 334.4 %all-to-all-start.1 = ((bf16[128,2,6144]{2,1,0:T(2,128)(2,1)}), bf16[128,2,6144]{2,1,0:T(2,128)(2,1)}, u32[]{:S(2)}, u32[]{:S(2)}) async-start(bf16[128,2,6144]{2,1,0:T(2,128)(2,1)} %reshape.786), calls=%async_computation.1 | async-start | bytes 6291456 | tf_op jit(solution)/shard_map/all_to_all | solution.py:149
  173.9 271.0 %collective-permute-start = (bf16[128,320]{1,0:T(8,128)(2,1)}, bf16[128,320]{1,0:T(8,128)(2,1)}, u32[]{:S(2)}, u32[]{:S(2)}) collective-permute-start(bf16[128,320]{1,0:T(8,128)(2,1)} %get-tuple-element.24), channel_id=1, source_target_pairs={{0,16},{4,20},{8,24},{12,28},{16,32},{20,36},{24,40},{28,44},{32,4... | collective-permute-start | bytes 245768 | tf_op jit(solution)/shard_map/ppermute | solution.py:18
  178.7 267.1 %collective-permute-start.1 = (bf16[128,320]{1,0:T(8,128)(2,1)}, bf16[128,320]{1,0:T(8,128)(2,1)}, u32[]{:S(2)}, u32[]{:S(2)}) collective-permute-start(bf16[128,320]{1,0:T(8,128)(2,1)} %get-tuple-element.23), channel_id=1, source_target_pairs={{0,12},{4,16},{8,20},{12,24},{16,28},{20,32},{24,36},{28,40},{32,4... | collective-permute-start | bytes 245768 | tf_op jit(solution)/shard_map/ppermute | solution.py:18
  182.3 264.4 %collective-permute-start.2 = (bf16[128,320]{1,0:T(8,128)(2,1)}, bf16[128,320]{1,0:T(8,128)(2,1)}, u32[]{:S(2)}, u32[]{:S(2)}) collective-permute-start(bf16[128,320]{1,0:T(8,128)(2,1)} %get-tuple-element.22), channel_id=1, source_target_pairs={{0,8},{4,12},{8,16},{12,20},{16,24},{20,28},{24,32},{28,36},{32,40... | collective-permute-start | bytes 245768 | tf_op jit(solution)/shard_map/ppermute | solution.py:18
  185.4 262.2 %collective-permute-start.3 = (bf16[128,320]{1,0:T(8,128)(2,1)}, bf16[128,320]{1,0:T(8,128)(2,1)}, u32[]{:S(2)}, u32[]{:S(2)}) collective-permute-start(bf16[128,320]{1,0:T(8,128)(2,1)} %get-tuple-element.13), channel_id=1, source_target_pairs={{0,4},{4,8},{8,12},{12,16},{16,20},{20,24},{24,28},{28,32},{32,36}... | collective-permute-start | bytes 245768 | tf_op jit(solution)/shard_map/ppermute | solution.py:18
  189.5 8.3 %copy-start.13 = (bf16[32,128]{1,0:T(8,128)(2,1)S(1)}, bf16[32,128]{1,0:T(8,128)(2,1)}, u32[]{:S(2)}) copy-start(bf16[32,128]{1,0:T(8,128)(2,1)} %param.15) | copy-start | bytes 24580
  406.3 2.8 copy-start.6
  448.6 2.6 copy-start.10
  485.2 8.0 %copy-start.11 = (bf16[8,64,128]{2,1,0:T(8,128)(2,1)S(1)}, bf16[8,64,128]{2,1,0:T(8,128)(2,1)}, u32[]{:S(2)}) copy-start(bf16[8,64,128]{2,1,0:T(8,128)(2,1)} %gather_fusion.4) | copy-start | bytes 393220
  535.9 5.1 copy-start.8
  541.0 2.9 copy-start.4
  545.8 2.2 copy-start.7
  548.1 5.4 copy-start.9
  553.5 5.7 %copy-start.1 = (bf16[192,192]{1,0:T(8,128)(2,1)S(1)}, bf16[192,192]{1,0:T(8,128)(2,1)}, u32[]{:S(2)}) copy-start(bf16[192,192]{1,0:T(8,128)(2,1)} %param.16) | copy-start | bytes 221188
where the time goes:
time: 570 us; the launch traced here: 560 us
  blocking collectives  241 us (42%)
  local copies, waits for them, and re-layouts  153 us (27%)
  waiting for transfers between devices  69.2 us (12%)
  other arithmetic  36.7 us (6%)
  starting transfers between devices  30.9 us (5%)
  matrix products  28.4 us (5%)
    all_gather x1, blocking collectives, sent_together(): lax.all_gather(both, axis, axis=dim, tiled=True)  206 us
    all_to_all x1, waiting for transfers between devices, body(): lax.all_to_all(out_values, 'ctx', split_axis=0, concat_axis=0, tiled=True)  69.2 us
    unnamed x39, local copies, waits for them, and re-layouts  55.8 us
    all_to_all x1, blocking collectives, body(): lax.all_to_all(requests.reshape(devices, per_owner), 'ctx', split_axis=0,...  35.1 us
    ppermute x4, starting transfers between devices, shifted(): return lax.ppermute(value, axis, pairs)  14.3 us
    all_to_all x1, local copies, waits for them, and re-layouts, body(): lax.all_to_all(out_keys, 'ctx', split_axis=0, concat_axis=0, tiled=True)  13.3 us
  transfers between devices with their start and end apart: 6, of which 1 were waited for; matrix products, arithmetic and copies ran while one was open for 23% of the time, Pallas kernels for 0%

commit v1 on v0

v1 whole, which is shorter than its diff:
```python
import functools

import jax
import jax.numpy as jnp
from jax import lax
from jax.experimental import pallas as pl
from jax.experimental.pallas import tpu as pltpu
from jax.sharding import PartitionSpec as P

HEADS = 16
DK = 192
DV = 128
CMP_BLOCK = 32
SEL_BLOCK = 64
QBLOCK = 16
TOPN = 16
TOKENS = 128
NZ, NX = 16, 4
CHIPS = NZ * NX
DEVICES = 2 * CHIPS
PR, QR = 128, 224
VAL, HI, CMP = 0, 128, 192
WIN = 320
P_HALF = ((0, 64), (64, 128))
Q_HALF = ((0, 112), (112, 224))
MESH = pl.DeviceIdType.MESH
SCALE2 = DK**-0.5 * 1.4426950408889634
BF, F32 = jnp.bfloat16, jnp.float32
VMEM_LIMIT = 56 * 2**20


def pooled(rows, gains, mixing):
    summed = jnp.sum(rows.astype(F32).reshape(4, CMP_BLOCK, rows.shape[1]) * gains.astype(F32)[None], axis=1)
    return summed


def compressed(rows_of, gains, mixing):
    both = jnp.concatenate([pooled(rows_of[r], gains, mixing) for r in (0, 1)], axis=0)
    return jnp.dot(both.astype(BF), mixing, preferred_element_type=F32)


def paired_high(k):
    return jnp.concatenate([k[0:64, 128:192], k[64:128, 128:192]], axis=1)


def gather_kernel(keys, values, pos_k, pos_v, mix_k, mix_v, gp, gq, win, mine_p, mine_q, span,
                  pz, qz, px, qx, d2d, send, lsem, wrecv, wsend):
    me = lax.axis_index("ctx")
    z, x, c = me // 8, (me // 2) % 4, me % 2
    chip = me // 2

    def dev(zz, xx):
        return ((zz + NZ) % NZ) * 8 + ((xx + NX) % NX) * 2 + c

    def slot(zz, xx):
        return c * CHIPS + ((zz + 2 * NZ) % NZ) * NX + (xx + NX) % NX

    def zrow(zz):
        return pl.ds(c * CHIPS + ((zz + 2 * NZ) % NZ) * NX, NX)

    zn = [dev(z + 1, x), dev(z - 1, x)]
    xn = [dev(z, x + 1), dev(z, x - 1)]
    other = me + 1 - 2 * c

    def chip_dev(offset):
        return (chip + offset + CHIPS) % CHIPS * 2 + c

    near = [chip_dev(o) for o in (1, 2, -1, -2)]
    bar = pltpu.get_barrier_semaphore()
    for d in (*zn, *xn, other, *near):
        pl.semaphore_signal(bar, inc=1, device_id={"ctx": d}, device_id_type=MESH)

    mine_p[...] = keys[0, :, 0:128]
    mine_q[VAL : VAL + 128] = values[0]
    mine_q[HI : HI + 64] = paired_high(keys[0])
    ck = compressed(keys, pos_k[...], mix_k[...])
    cv = compressed(values, pos_v[...], mix_v[...])
    mine_q[CMP : CMP + 16] = jnp.concatenate([ck[:, 0:128], cv], axis=0).astype(BF)
    hi = jnp.concatenate([ck[:, 128:192], jnp.zeros((8, 64), F32)], axis=1)
    mine_q[CMP + 16 : CMP + 32] = jnp.concatenate([hi, jnp.zeros((8, 128), F32)], axis=0).astype(BF)
    for r in (0, 1):
        span[r, 0:128] = keys[r, :, 0:128]
        span[r, 128:256] = values[r]
        span[r, 256:320] = paired_high(keys[r])
    me_s = slot(z, x)
    local = [
        pltpu.make_async_copy(mine_p, gp.at[me_s], lsem.at[0]),
        pltpu.make_async_copy(mine_q, gq.at[me_s], lsem.at[1]),
        pltpu.make_async_copy(span.at[1], win.at[c], lsem.at[2]),
    ]
    for cp in local:
        cp.start()
    for cp in local:
        cp.wait()
    pl.semaphore_wait(bar, 9)

    def remote(ref, d, ss, rs, dst=None):
        return pltpu.make_async_remote_copy(
            src_ref=ref, dst_ref=ref if dst is None else dst, send_sem=ss, recv_sem=rs,
            device_id={"ctx": d}, device_id_type=MESH,
        )

    def part(buf, s, rows):
        return buf.at[s] if rows is None else buf.at[s, rows[0] : rows[1]]

    def sp(s, rows, d, rs):
        remote(part(gp, s, rows), d, send.at[0], rs).start()

    def sq(s, rows, d, rs):
        remote(part(gq, s, rows), d, send.at[1], rs).start()

    def wp(s, rows, rs):
        remote(part(gp, s, rows), other, send.at[0], rs).wait_recv()

    def wq(s, rows, rs):
        remote(part(gq, s, rows), other, send.at[1], rs).wait_recv()

    def zsend_p(zz, r, d, k, half):
        sp(slot(zz, x + r), P_HALF[d] if half else None, zn[d], pz.at[d, k, r])

    def zsend_q(zz, d, k, half):
        sq(slot(zz, x), Q_HALF[d] if half else None, zn[d], qz.at[d, k])

    def xsend_q(zz, t):
        for d in (0, 1):
            sq(slot(zz, x), None, xn[d], qx.at[t, d])

    def d2d_p(zz):
        remote(gp.at[zrow(zz)], other, send.at[2], d2d.at[0]).start()

    def d2d_q(zz):
        remote(gq.at[zrow(zz)], other, send.at[3], d2d.at[1]).start()

    for d in (0, 1):
        sp(me_s, None, xn[d], px.at[d])
    for d in (0, 1):
        zsend_q(z, d, 1, False)
    for d in (0, 1):
        zsend_p(z, 0, d, 1, False)
    xsend_q(z, 0)
    for o in (1, 2):
        wrapped = jnp.where(chip + o >= CHIPS, 0, 1)
        remote(span.at[wrapped], near[o - 1], wsend.at[o], wrecv.at[o], win.at[2 * o + c]).start()
    remote(win.at[c], other, wsend.at[0], wrecv.at[0]).start()
    for d, r in ((0, 3), (1, 1)):
        wp(slot(z, x + r), None, px.at[d])
        sp(slot(z, x + r), P_HALF[d], xn[d], px.at[2 + d])
        for e in (0, 1):
            zsend_p(z, r, e, 1, False)
    for d in (0, 1):
        wp(slot(z, x + 2), P_HALF[d], px.at[2 + d])
    for e in (0, 1):
        zsend_p(z, 2, e, 1, False)
    d2d_p(z)

    def qx_full(zz, t):
        for d, r in ((0, 3), (1, 1)):
            wq(slot(zz, x + r), None, qx.at[t, d])
            sq(slot(zz, x + r), Q_HALF[d], xn[d], qx.at[t, 2 + d])

    def qx_half(zz, t):
        for d in (0, 1):
            wq(slot(zz, x + 2), Q_HALF[d], qx.at[t, 2 + d])
        d2d_q(zz)

    def at_z(d, k):
        return z - k if d == 0 else z + k

    def at_t(d, k):
        return k if d == 0 else 8 + k

    def step(k, last):
        for d in (0, 1):
            wq(slot(at_z(d, k), x), None, qz.at[d, k])
            zsend_q(at_z(d, k), d, k + 1, last)
            xsend_q(at_z(d, k), at_t(d, k))
        for r in (0, 3, 1, 2):
            for d in (0, 1):
                wp(slot(at_z(d, k), x + r), None, pz.at[d, k, r])
                zsend_p(at_z(d, k), r, d, k + 1, last)
        for d in (0, 1):
            d2d_p(at_z(d, k))

    def lag1(k):
        for d in (0, 1):
            qx_full(at_z(d, k), at_t(d, k))

    def lag2(k):
        for d in (0, 1):
            qx_half(at_z(d, k), at_t(d, k))

    step(1, False)
    qx_full(z, 0)
    step(2, False)
    lag1(1)
    qx_half(z, 0)
    for o in (1, 2):
        remote(win.at[2 * o + c], other, wsend.at[o], wrecv.at[o]).wait_recv()
        remote(win.at[2 * o + c], other, wsend.at[2 + o], wrecv.at[2 + o]).start()

    def loop(k, carry):
        step(k, False)
        lag1(k - 1)
        lag2(k - 2)
        return carry

    lax.fori_loop(3, 7, loop, 0)
    step(7, True)
    lag1(6)
    lag2(5)
    for d in (0, 1):
        wq(slot(z - 8, x), Q_HALF[d], qz.at[d, 8])
    xsend_q(z - 8, 8)
    for r in (0, 3, 1, 2):
        for d in (0, 1):
            wp(slot(z - 8, x + r), P_HALF[d], pz.at[d, 8, r])
    d2d_p(z - 8)
    lag1(7)
    lag2(6)
    qx_full(z - 8, 8)
    lag2(7)
    qx_half(z - 8, 8)
    theirs = pl.ds((1 - c) * CHIPS, CHIPS)
    for n, buf in enumerate((gp, gq)):
        remote(buf.at[theirs], other, send.at[2 + n], d2d.at[n]).wait_recv()
    for o in (0, 1, 2):
        ref = win.at[2 * o + 1 - c]
        remote(ref, other, wsend.at[0], wrecv.at[o if o == 0 else 2 + o]).wait_recv()
    for n, buf in enumerate((gp, gq)):
        remote(buf.at[0 : CHIPS - 1], other, send.at[n], d2d.at[n]).wait_send()
        remote(buf.at[0:CHIPS], other, send.at[2 + n], d2d.at[n]).wait_send()
    for i in range(5):
        remote(win.at[0], other, wsend.at[i], wrecv.at[0]).wait_send()


def gather(keys, values, pos_k, pos_v, mix_k, mix_v):
    dma = pltpu.SemaphoreType.DMA
    shapes = [(DEVICES, PR, 128), (DEVICES, QR, 128), (6, WIN, 128)]
    return pl.pallas_call(
        gather_kernel,
        out_shape=[jax.ShapeDtypeStruct(s, BF) for s in shapes],
        in_specs=[pl.BlockSpec(memory_space=pltpu.VMEM)] * 6,
        out_specs=[pl.BlockSpec(memory_space=pl.ANY)] * 3,
        scratch_shapes=[
            pltpu.VMEM((PR, 128), BF),
            pltpu.VMEM((QR, 128), BF),
            pltpu.VMEM((2, WIN, 128), BF),
            dma((2, 9, 4)),
            dma((2, 9)),
            dma((4,)),
            dma((NZ, 4)),
            dma((2,)),
            dma((4,)),
            dma((3,)),
            dma((5,)),
            dma((5,)),
        ],
        compiler_params=pltpu.CompilerParams(
            collective_id=0, has_side_effects=True, vmem_limit_bytes=24 * 2**20
        ),
    )(keys, values, pos_k, pos_v, mix_k, mix_v)


def mixed(query_rows, key_rows, value_rows, bias):
    heads, tokens = query_rows.shape[0], query_rows.shape[1]
    count = key_rows.shape[0]
    scores = lax.dot_general(
        query_rows.reshape(heads * tokens, 256), key_rows, (((1,), (1,)), ((), ())), preferred_element_type=F32
    )
    scores = scores.reshape(heads, tokens, count) + bias[None]
    highest = jnp.max(scores, axis=2, keepdims=True)
    weights = jnp.exp2((scores - highest) * SCALE2).astype(BF)
    both = jnp.dot(weights.reshape(heads * tokens, count), value_rows, preferred_element_type=F32)
    return (both[:, 0:128] / both[:, 128:256]).reshape(heads, tokens, DV)


def prepare(q, gates, qs, gate_rows, vx):
    none = jnp.zeros((TOKENS, 64), BF)
    for h in range(HEADS):
        qs[h] = jnp.concatenate([q[:, h * DK : (h + 1) * DK], none], axis=1)
    g = jax.nn.sigmoid(gates[...].astype(F32))
    for i in range(3 * HEADS):
        gate_rows[i] = jnp.broadcast_to(g[:, i : i + 1], (TOKENS, DV))
    vx[:, 128:256] = jnp.ones((vx.shape[0], 128), BF)


def window_part(win, qs, gate_rows, acc, kx, vx, bias, c):
    for i in range(5):
        back = 4 - i - c
        off = (back + 1) // 2
        core = (2 * off - back) % 2
        piece = 2 * off + core
        rows = slice(128 * i, 128 * (i + 1))
        kx[rows, 0:128] = win[piece, 0:128]
        vx[rows, 0:128] = win[piece, 128:256]
        high = win[piece, 256:320]
        kx[128 * i : 128 * i + 64, 128:256] = high
        kx[128 * i + 64 : 128 * i + 128, 128:256] = pltpu.roll(high, 64, 1)
    count = 5 * TOKENS
    column = lax.broadcasted_iota(jnp.int32, (TOKENS, count), 1)
    token = lax.broadcasted_iota(jnp.int32, (TOKENS, count), 0)
    inside = (column > token) & (column <= 4 * TOKENS + token)
    bias[:, 0:count] = jnp.where(inside, 0.0, -jnp.inf)

    def heads(i, carry):
        at = pl.ds(2 * i, 2)
        o = mixed(qs[at], kx[0:count], vx[0:count], bias[:, 0:count])
        acc[at] = o * gate_rows[pl.ds(2 * HEADS + 2 * i, 2)]
        return carry

    lax.fori_loop(0, HEADS // 2, heads, 0)


def compressed_part(gq, qs, gate_rows, acc, kx, vx, bias, me):
    tile = gq[:, CMP : CMP + 16].astype(F32)
    count = DEVICES * 8
    kx[:, 0:128] = tile[:, 0:8].reshape(count, 128).astype(BF)
    vx[:, 0:128] = tile[:, 8:16].reshape(count, 128).astype(BF)
    kx[:, 128:256] = gq[:, CMP + 16 : CMP + 32].astype(F32)[:, 0:8].reshape(count, 128).astype(BF)
    column = lax.broadcasted_iota(jnp.int32, (TOKENS, count), 1)
    token = lax.broadcasted_iota(jnp.int32, (TOKENS, count), 0)
    where = column // 8
    holder = where % CHIPS * 2 + where // CHIPS
    within = column % 8
    end = jnp.where(within < 4, 0, (holder - me) * TOKENS + (within - 3) * CMP_BLOCK - 1)
    bias[...] = jnp.where(end <= token, 0.0, -jnp.inf)

    def heads(i, carry):
        at = pl.ds(2 * i, 2)
        o = mixed(qs[at], kx[...], vx[...], bias[...])
        acc[at] += o * gate_rows[at]
        return carry

    lax.fori_loop(0, HEADS // 2, heads, 0)


def selected_part(sel, gp, gq, win, qs, gate_rows, acc, kx, vx, out, c):
    count = TOPN * SEL_BLOCK

    def group(g, carry):
        mine = g // 4
        kx[0:64, 0:128] = win[c, pl.ds(pl.multiple_of(mine * 64, 64), 64)]
        vx[0:64, 0:128] = win[c, pl.ds(pl.multiple_of(128 + mine * 64, 64), 64)]
        high = win[c, 256:320]
        kx[0:64, 128:256] = jnp.where(mine == 1, pltpu.roll(high, 64, 1), high)
        for e in range(1, TOPN):
            block = jnp.maximum(sel[g, e], 0)
            piece, odd = block // 2, block % 2
            s = piece % 2 * CHIPS + piece // 2
            first = pl.multiple_of(odd * 64, 64)
            rows = slice(64 * e, 64 * (e + 1))
            kx[rows, 0:128] = gp[s, pl.ds(first, 64)]
            vx[rows, 0:128] = gq[s, pl.ds(first, 64)]
            high = gq[s, HI : HI + 64]
            kx[rows, 128:256] = jnp.where(odd == 1, pltpu.roll(high, 64, 1), high)
        column = lax.broadcasted_iota(jnp.int32, (QBLOCK, count), 1)
        token = lax.broadcasted_iota(jnp.int32, (QBLOCK, count), 0)
        bad = (column < SEL_BLOCK) & (column > (g % 4) * QBLOCK + token)
        for e in range(1, TOPN):
            bad = bad | ((column // SEL_BLOCK == e) & (sel[g, e] < 0))
        bias = jnp.where(bad, -jnp.inf, 0.0)
        rows = pl.ds(pl.multiple_of(g * QBLOCK, QBLOCK), QBLOCK)
        o = mixed(qs[:, rows], kx[...], vx[...], bias)
        o = acc[:, rows] + o * gate_rows[HEADS : 2 * HEADS, rows]
        for h in range(HEADS):
            out[rows, h * DV : (h + 1) * DV] = o[h].astype(BF)
        return carry

    lax.fori_loop(0, QBLOCK // 2, group, 0)


def attend_kernel(sel, q, gates, gp, gq, win, out, qs, gate_rows, acc, kx, vx, bias):
    me = lax.axis_index("ctx")
    c = me % 2
    prepare(q, gates, qs, gate_rows, vx)
    window_part(win, qs, gate_rows, acc, kx, vx, bias, c)
    compressed_part(gq, qs, gate_rows, acc, kx, vx, bias, me)
    selected_part(sel, gp, gq, win, qs, gate_rows, acc, kx, vx, out, c)


def attend(sel_ids, queries, gate_logits, gp, gq, win):
    vmem = pl.BlockSpec(memory_space=pltpu.VMEM)
    return pl.pallas_call(
        attend_kernel,
        out_shape=jax.ShapeDtypeStruct((TOKENS, HEADS * DV), BF),
        in_specs=[pl.BlockSpec(memory_space=pltpu.SMEM)] + [vmem] * 5,
        out_specs=vmem,
        scratch_shapes=[
            pltpu.VMEM((HEADS, TOKENS, 256), BF),
            pltpu.VMEM((3 * HEADS, TOKENS, DV), F32),
            pltpu.VMEM((HEADS, TOKENS, DV), F32),
            pltpu.VMEM((1024, 256), BF),
            pltpu.VMEM((1024, 256), BF),
            pltpu.VMEM((TOKENS, 1024), F32),
        ],
        compiler_params=pltpu.CompilerParams(vmem_limit_bytes=VMEM_LIMIT),
    )(sel_ids, queries, gate_logits, gp, gq, win)


def body(queries, keys, values, gate_logits, sel_ids, pos_k, pos_v, mix_k, mix_v):
    gp, gq, win = gather(keys, values, pos_k, pos_v, mix_k, mix_v)
    return attend(sel_ids, queries, gate_logits, gp, gq, win)


def solution(mesh):
    in_specs = (
        P("ctx", "grp"),
        P(None, "ctx", "grp"),
        P(None, "ctx", "grp"),
        P("ctx", "grp"),
        P("ctx", "grp"),
        P(None, "grp"),
        P(None, "grp"),
        P(None, "grp"),
        P(None, "grp"),
    )
    return jax.shard_map(body, mesh=mesh, in_specs=in_specs, out_specs=P("ctx", "grp"), check_vma=False)
```

time: 570 us -> 99.7 us (0.17); the launches traced: 560 us -> 99.3 us
  blocking collectives: 241 us -> 0 us
  local copies, waits for them, and re-layouts: 153 us -> 12.1 us
  Pallas kernels: 0 us -> 87.2 us
  waiting for transfers between devices: 69.2 us -> 0 us
  other arithmetic: 36.7 us -> 0 us
  starting transfers between devices: 30.9 us -> 0 us
  matrix products: 28.4 us -> 0 us
    all_gather x1 -> x0, blocking collectives: 206 us -> none  [sent_together(): lax.all_gather(both, axis, axis=dim, tiled=True)]
    pallas_call x0 -> x2, Pallas kernels: none -> 87.2 us  [the longest x1 59.6 us: gather(): pl.pallas_call(gather_kernel, out_shape=[jax.ShapeDtypeStruct(s, BF) for...]
    all_to_all x2 -> x0, waiting for transfers between devices: 69.2 us -> none  [the longest x1 69.2 us: body(): lax.all_to_all(out_values, 'ctx', split_axis=0, concat_axis=0, tiled=True)]
    unnamed x39 -> x18, local copies, waits for them, and re-layouts: 55.8 us -> 12.1 us
    all_to_all x1 -> x0, blocking collectives: 35.1 us -> none  [body(): lax.all_to_all(requests.reshape(devices, per_owner), 'ctx', split_axis=0,...]
    gather x9 -> x0, local copies, waits for them, and re-layouts: 28.4 us -> none  [the longest x2 9.43 us: body(): out_keys = key_blocks[chosen].reshape(devices, per_owner, SEL_BLOCK * DK)]
    dot_general x10 -> x0, matrix products: 28.4 us -> none  [the longest x2 9.77 us: body(): jnp.dot(weights.astype(jnp.bfloat16).reshape(tokens * HEADS, high_row - l...]
    all_to_all x3 -> x0, local copies, waits for them, and re-layouts: 22.6 us -> none  [the longest x1 13.3 us: body(): lax.all_to_all(out_keys, 'ctx', split_axis=0, concat_axis=0, tiled=True)]
  transfers between devices with their start and end apart: 6 -> 0, of which waited for: 1 -> 0; matrix products, arithmetic and copies ran while one was open for 23% -> 0% of each run, Pallas kernels for 0% -> 0%
where the time goes in v1:
time: 99.7 us; the launch traced here: 99.3 us
  Pallas kernels  87.2 us (87%)
  local copies, waits for them, and re-layouts  12.1 us (12%)
    pallas_call x1, Pallas kernels, gather(): pl.pallas_call(gather_kernel, out_shape=[jax.ShapeDtypeStruct(s, BF) for...  59.6 us
    pallas_call x1, Pallas kernels, attend(): pl.pallas_call(attend_kernel, out_shape=jax.ShapeDtypeStruct((TOKENS, HEA...  27.6 us
    unnamed x18, local copies, waits for them, and re-layouts  12.1 us

profile of v1, /device:TPU:1, one launch (start us, length us, event | category | flops | bytes accessed | tf_op | source)
XLA Modules:
  0.0 99.3 jit_solution(12575002917161339310)
XLA Ops:
  0.0 1.4 %copy.11.gates = bf16[128,48]{1,0:T(8,128)(2,1)} copy(bf16[128,48]{0,1:T(8,128)(2,1)} %param.12) | data formatting | bytes 24576 | tf_op args[3]
  1.4 1.0 %copy.10.keys = bf16[2,128,192]{2,1,0:T(8,128)(2,1)S(1)} copy(bf16[2,128,192]{1,2,0:T(8,128)(2,1)} %param.10) | data formatting | bytes 196608 | tf_op args[1]
  2.4 0.0 copy-start.3
  2.4 0.9 copy-done.3
  3.3 0.0 copy-start.4
  3.3 0.8 copy-done.4
  4.2 0.0 copy-start.5
  4.2 0.8 copy-done.5
  4.9 0.0 copy-start.6
  4.9 0.7 copy-done.6
  5.6 0.0 copy-start.7
  5.6 0.7 copy-done.7
  6.3 59.6 %shard_map.91 = (bf16[128,128,128]{2,1,0:T(8,128)(2,1)S(1)}, bf16[128,224,128]{2,1,0:T(8,128)(2,1)S(1)}, bf16[6,320,128]{2,1,0:T(8,128)(2,1)S(1)}) custom-call(bf16[2,128,192]{2,1,0:T(8,128)(2,1)S(1)} %copy.10.keys, bf16[2,128,128]{2,1,0:T(8,128)(2,1)S(1)} %copy-done.4, bf16[32,192]{1,0:T(8,128)(2,1)S(1)} %copy-done.6, bf16[32,128]{1,0:T(8,128)(2,1)S(1)} %copy-done.7, ...), custom_call_target="tpu_custom_call" | custom-call | tf_op jit(solution)/shard_map/pallas_call | solution.py:239
  65.9 0.0 copy-start
  65.9 2.9 %copy-done = bf16[128,224,128]{2,1,0:T(8,128)(2,1)} copy-done((bf16[128,224,128]{2,1,0:T(8,128)(2,1)}, bf16[128,224,128]{2,1,0:T(8,128)(2,1)S(1)}, u32[]{:S(2)}) %copy-start) | copy-done | bytes 7340056
  68.9 0.0 copy-start.1
  68.9 2.1 %copy-done.1 = bf16[128,128,128]{2,1,0:T(8,128)(2,1)} copy-done((bf16[128,128,128]{2,1,0:T(8,128)(2,1)}, bf16[128,128,128]{2,1,0:T(8,128)(2,1)S(1)}, u32[]{:S(2)}) %copy-start.1) | copy-done | bytes 4194328
  70.9 0.0 copy-start.2
  70.9 0.8 copy-done.2
  71.7 27.6 %shard_map.92 = bf16[128,2048]{1,0:T(8,128)(2,1)} custom-call(s32[8,16]{1,0:T(8,128)} %sel.1, bf16[128,3072]{1,0:T(8,128)(2,1)} %q.1, bf16[128,48]{1,0:T(8,128)(2,1)} %copy.11.gates, bf16[128,128,128]{2,1,0:T(8,128)(2,1)} %copy-done.1, bf16[128,224,128]{2,1,0:T(8,128)(2,1)} %copy-done, bf16[6,320,128]{2,1,0:T(8,128)(2,1)} %copy-done.2), custom_call_target="tpu_custom_call" | custom-call | tf_op jit(solution)/shard_map/pallas_call | solution.py:383
Async XLA Ops:
  2.4 0.9 copy-start.3
  3.3 0.8 copy-start.4
  4.2 0.8 copy-start.5
  4.9 0.7 copy-start.6
  5.6 0.7 copy-start.7
  65.9 2.9 %copy-start = (bf16[128,224,128]{2,1,0:T(8,128)(2,1)}, bf16[128,224,128]{2,1,0:T(8,128)(2,1)S(1)}, u32[]{:S(2)}) copy-start(bf16[128,224,128]{2,1,0:T(8,128)(2,1)S(1)} %get-tuple-element.9.gq) | copy-start | bytes 22020100
  68.9 2.1 %copy-start.1 = (bf16[128,128,128]{2,1,0:T(8,128)(2,1)}, bf16[128,128,128]{2,1,0:T(8,128)(2,1)S(1)}, u32[]{:S(2)}) copy-start(bf16[128,128,128]{2,1,0:T(8,128)(2,1)S(1)} %get-tuple-element.8.gp) | copy-start | bytes 12582916
  70.9 0.8 copy-start.2

commit v2 on v1

--- a/solution.py
+++ b/solution.py
@@ -43,8 +43,10 @@
     return jnp.concatenate([k[0:64, 128:192], k[64:128, 128:192]], axis=1)
 
 
-def gather_kernel(keys, values, pos_k, pos_v, mix_k, mix_v, gp, gq, win, mine_p, mine_q, span,
-                  pz, qz, px, qx, d2d, send, lsem, wrecv, wsend):
+def fused_kernel(sel, q_in, keys_in, values_in, gates_in, pos_k_in, pos_v_in, mix_k_in, mix_v_in, out,
+                 q, keys, values, gates, pos_k, pos_v, mix_k, mix_v,
+                 gp, gq, win, span, qs, gate_rows, acc, kx, vx, bias,
+                 pz, qz, px, qx, d2d, send, lsem, wrecv, wsend):
     me = lax.axis_index("ctx")
     z, x, c = me // 8, (me // 2) % 4, me % 2
     chip = me // 2
@@ -66,32 +68,31 @@
         return (chip + offset + CHIPS) % CHIPS * 2 + c
 
     near = [chip_dev(o) for o in (1, 2, -1, -2)]
+    ins = (keys_in, values_in, pos_k_in, pos_v_in, mix_k_in, mix_v_in, gates_in, q_in)
+    staged = (keys, values, pos_k, pos_v, mix_k, mix_v, gates, q)
+    local = [pltpu.make_async_copy(r, v, lsem.at[i]) for i, (r, v) in enumerate(zip(ins, staged))]
+    for cp in local:
+        cp.start()
     bar = pltpu.get_barrier_semaphore()
     for d in (*zn, *xn, other, *near):
         pl.semaphore_signal(bar, inc=1, device_id={"ctx": d}, device_id_type=MESH)
-
-    mine_p[...] = keys[0, :, 0:128]
-    mine_q[VAL : VAL + 128] = values[0]
-    mine_q[HI : HI + 64] = paired_high(keys[0])
-    ck = compressed(keys, pos_k[...], mix_k[...])
+    for cp in local[:6]:
+        cp.wait()
+    me_s = slot(z, x)
+    rows = [keys[r].astype(F32).T.astype(BF) for r in (0, 1)]
+    for r in (0, 1):
+        span[r, 0:128] = rows[r][:, 0:128]
+        span[r, 128:256] = values[r]
+        span[r, 256:320] = paired_high(rows[r])
+    gp[me_s] = span[0, 0:128]
+    gq[me_s, VAL : VAL + 128] = values[0]
+    gq[me_s, HI : HI + 64] = span[0, 256:320]
+    ck = compressed(rows, pos_k[...], mix_k[...])
     cv = compressed(values, pos_v[...], mix_v[...])
-    mine_q[CMP : CMP + 16] = jnp.concatenate([ck[:, 0:128], cv], axis=0).astype(BF)
+    gq[me_s, CMP : CMP + 16] = jnp.concatenate([ck[:, 0:128], cv], axis=0).astype(BF)
     hi = jnp.concatenate([ck[:, 128:192], jnp.zeros((8, 64), F32)], axis=1)
-    mine_q[CMP + 16 : CMP + 32] = jnp.concatenate([hi, jnp.zeros((8, 128), F32)], axis=0).astype(BF)
-    for r in (0, 1):
-        span[r, 0:128] = keys[r, :, 0:128]
-        span[r, 128:256] = values[r]
-        span[r, 256:320] = paired_high(keys[r])
-    me_s = slot(z, x)
-    local = [
-        pltpu.make_async_copy(mine_p, gp.at[me_s], lsem.at[0]),
-        pltpu.make_async_copy(mine_q, gq.at[me_s], lsem.at[1]),
-        pltpu.make_async_copy(span.at[1], win.at[c], lsem.at[2]),
-    ]
-    for cp in local:
-        cp.start()
-    for cp in local:
-        cp.wait()
+    gq[me_s, CMP + 16 : CMP + 32] = jnp.concatenate([hi, jnp.zeros((8, 128), F32)], axis=0).astype(BF)
+    win[c] = span[1]
     pl.semaphore_wait(bar, 9)
 
     def remote(ref, d, ss, rs, dst=None):
@@ -152,6 +153,9 @@
     for e in (0, 1):
         zsend_p(z, 2, e, 1, False)
     d2d_p(z)
+    for cp in local[6:]:
+        cp.wait()
+    prepare(q, gates, qs, gate_rows, vx)
 
     def qx_full(zz, t):
         for d, r in ((0, 3), (1, 1)):
@@ -198,9 +202,16 @@
         remote(win.at[2 * o + c], other, wsend.at[o], wrecv.at[o]).wait_recv()
         remote(win.at[2 * o + c], other, wsend.at[2 + o], wrecv.at[2 + o]).start()
 
+    for o in (0, 1, 2):
+        ref = win.at[2 * o + 1 - c]
+        remote(ref, other, wsend.at[0], wrecv.at[o if o == 0 else 2 + o]).wait_recv()
+    window_keys(win, kx, vx, bias, c)
+
     def loop(k, carry):
         step(k, False)
+        window_heads(2 * (k - 3), qs, gate_rows, acc, kx, vx, bias)
         lag1(k - 1)
+        window_heads(2 * (k - 3) + 1, qs, gate_rows, acc, kx, vx, bias)
         lag2(k - 2)
         return carry
 
@@ -223,42 +234,13 @@
     theirs = pl.ds((1 - c) * CHIPS, CHIPS)
     for n, buf in enumerate((gp, gq)):
         remote(buf.at[theirs], other, send.at[2 + n], d2d.at[n]).wait_recv()
-    for o in (0, 1, 2):
-        ref = win.at[2 * o + 1 - c]
-        remote(ref, other, wsend.at[0], wrecv.at[o if o == 0 else 2 + o]).wait_recv()
+    compressed_part(gq, qs, gate_rows, acc, kx, vx, bias, me)
+    selected_part(sel, gp, gq, win, qs, gate_rows, acc, kx, vx, out, c)
     for n, buf in enumerate((gp, gq)):
         remote(buf.at[0 : CHIPS - 1], other, send.at[n], d2d.at[n]).wait_send()
         remote(buf.at[0:CHIPS], other, send.at[2 + n], d2d.at[n]).wait_send()
     for i in range(5):
         remote(win.at[0], other, wsend.at[i], wrecv.at[0]).wait_send()
-
-
-def gather(keys, values, pos_k, pos_v, mix_k, mix_v):
-    dma = pltpu.SemaphoreType.DMA
-    shapes = [(DEVICES, PR, 128), (DEVICES, QR, 128), (6, WIN, 128)]
-    return pl.pallas_call(
-        gather_kernel,
-        out_shape=[jax.ShapeDtypeStruct(s, BF) for s in shapes],
-        in_specs=[pl.BlockSpec(memory_space=pltpu.VMEM)] * 6,
-        out_specs=[pl.BlockSpec(memory_space=pl.ANY)] * 3,
-        scratch_shapes=[
-            pltpu.VMEM((PR, 128), BF),
-            pltpu.VMEM((QR, 128), BF),
-            pltpu.VMEM((2, WIN, 128), BF),
-            dma((2, 9, 4)),
-            dma((2, 9)),
-            dma((4,)),
-            dma((NZ, 4)),
-            dma((2,)),
-            dma((4,)),
-            dma((3,)),
-            dma((5,)),
-            dma((5,)),
-        ],
-        compiler_params=pltpu.CompilerParams(
-            collective_id=0, has_side_effects=True, vmem_limit_bytes=24 * 2**20
-        ),
-    )(keys, values, pos_k, pos_v, mix_k, mix_v)
 
 
 def mixed(query_rows, key_rows, value_rows, bias):
@@ -278,13 +260,13 @@
     none = jnp.zeros((TOKENS, 64), BF)
     for h in range(HEADS):
         qs[h] = jnp.concatenate([q[:, h * DK : (h + 1) * DK], none], axis=1)
-    g = jax.nn.sigmoid(gates[...].astype(F32))
+    g = jax.nn.sigmoid(gates[...].astype(F32)).T
     for i in range(3 * HEADS):
         gate_rows[i] = jnp.broadcast_to(g[:, i : i + 1], (TOKENS, DV))
     vx[:, 128:256] = jnp.ones((vx.shape[0], 128), BF)
 
 
-def window_part(win, qs, gate_rows, acc, kx, vx, bias, c):
+def window_keys(win, kx, vx, bias, c):
     for i in range(5):
         back = 4 - i - c
         off = (back + 1) // 2
@@ -302,13 +284,12 @@
     inside = (column > token) & (column <= 4 * TOKENS + token)
     bias[:, 0:count] = jnp.where(inside, 0.0, -jnp.inf)
 
-    def heads(i, carry):
-        at = pl.ds(2 * i, 2)
-        o = mixed(qs[at], kx[0:count], vx[0:count], bias[:, 0:count])
-        acc[at] = o * gate_rows[pl.ds(2 * HEADS + 2 * i, 2)]
-        return carry
-
-    lax.fori_loop(0, HEADS // 2, heads, 0)
+
+def window_heads(i, qs, gate_rows, acc, kx, vx, bias):
+    count = 5 * TOKENS
+    at = pl.ds(2 * i, 2)
+    o = mixed(qs[at], kx[0:count], vx[0:count], bias[:, 0:count])
+    acc[at] = o * gate_rows[pl.ds(2 * HEADS + 2 * i, 2)]
 
 
 def compressed_part(gq, qs, gate_rows, acc, kx, vx, bias, me):
@@ -345,19 +326,20 @@
         kx[0:64, 128:256] = jnp.where(mine == 1, pltpu.roll(high, 64, 1), high)
         for e in range(1, TOPN):
             block = jnp.maximum(sel[g, e], 0)
-            piece, odd = block // 2, block % 2
-            s = piece % 2 * CHIPS + piece // 2
-            first = pl.multiple_of(odd * 64, 64)
+            odd = block & 1
+            s = ((block >> 1) & 1) * CHIPS + (block >> 2)
+            second = jnp.broadcast_to(odd, (64, 128)) == 1
+            low, rest = gp[s], gq[s]
+            high = rest[HI : HI + 64]
             rows = slice(64 * e, 64 * (e + 1))
-            kx[rows, 0:128] = gp[s, pl.ds(first, 64)]
-            vx[rows, 0:128] = gq[s, pl.ds(first, 64)]
-            high = gq[s, HI : HI + 64]
-            kx[rows, 128:256] = jnp.where(odd == 1, pltpu.roll(high, 64, 1), high)
+            kx[rows, 0:128] = jnp.where(second, low[64:128], low[0:64])
+            vx[rows, 0:128] = jnp.where(second, rest[64:128], rest[0:64])
+            kx[rows, 128:256] = jnp.where(second, pltpu.roll(high, 64, 1), high)
         column = lax.broadcasted_iota(jnp.int32, (QBLOCK, count), 1)
         token = lax.broadcasted_iota(jnp.int32, (QBLOCK, count), 0)
         bad = (column < SEL_BLOCK) & (column > (g % 4) * QBLOCK + token)
         for e in range(1, TOPN):
-            bad = bad | ((column // SEL_BLOCK == e) & (sel[g, e] < 0))
+            bad = bad | ((column // SEL_BLOCK == e) & (jnp.broadcast_to(sel[g, e], (QBLOCK, count)) < 0))
         bias = jnp.where(bad, -jnp.inf, 0.0)
         rows = pl.ds(pl.multiple_of(g * QBLOCK, QBLOCK), QBLOCK)
         o = mixed(qs[:, rows], kx[...], vx[...], bias)
@@ -369,37 +351,43 @@
     lax.fori_loop(0, QBLOCK // 2, group, 0)
 
 
-def attend_kernel(sel, q, gates, gp, gq, win, out, qs, gate_rows, acc, kx, vx, bias):
-    me = lax.axis_index("ctx")
-    c = me % 2
-    prepare(q, gates, qs, gate_rows, vx)
-    window_part(win, qs, gate_rows, acc, kx, vx, bias, c)
-    compressed_part(gq, qs, gate_rows, acc, kx, vx, bias, me)
-    selected_part(sel, gp, gq, win, qs, gate_rows, acc, kx, vx, out, c)
-
-
-def attend(sel_ids, queries, gate_logits, gp, gq, win):
-    vmem = pl.BlockSpec(memory_space=pltpu.VMEM)
+def body(queries, keys, values, gate_logits, sel_ids, pos_k, pos_v, mix_k, mix_v):
+    dma = pltpu.SemaphoreType.DMA
+    turned = (
+        queries, keys.transpose(0, 2, 1), values, gate_logits.transpose(1, 0), pos_k, pos_v, mix_k, mix_v
+    )
+    anywhere = pl.BlockSpec(memory_space=pl.ANY)
     return pl.pallas_call(
-        attend_kernel,
+        fused_kernel,
         out_shape=jax.ShapeDtypeStruct((TOKENS, HEADS * DV), BF),
-        in_specs=[pl.BlockSpec(memory_space=pltpu.SMEM)] + [vmem] * 5,
-        out_specs=vmem,
+        in_specs=[pl.BlockSpec(memory_space=pltpu.SMEM)] + [anywhere] * 8,
+        out_specs=pl.BlockSpec(memory_space=pltpu.VMEM),
         scratch_shapes=[
+            *(pltpu.VMEM(a.shape, BF) for a in turned),
+            pltpu.VMEM((DEVICES, PR, 128), BF),
+            pltpu.VMEM((DEVICES, QR, 128), BF),
+            pltpu.VMEM((6, WIN, 128), BF),
+            pltpu.VMEM((2, WIN, 128), BF),
             pltpu.VMEM((HEADS, TOKENS, 256), BF),
             pltpu.VMEM((3 * HEADS, TOKENS, DV), F32),
             pltpu.VMEM((HEADS, TOKENS, DV), F32),
             pltpu.VMEM((1024, 256), BF),
             pltpu.VMEM((1024, 256), BF),
             pltpu.VMEM((TOKENS, 1024), F32),
+            dma((2, 9, 4)),
+            dma((2, 9)),
+            dma((4,)),
+            dma((NZ, 4)),
+            dma((2,)),
+            dma((4,)),
+            dma((8,)),
+            dma((5,)),
+            dma((5,)),
         ],
-        compiler_params=pltpu.CompilerParams(vmem_limit_bytes=VMEM_LIMIT),
-    )(sel_ids, queries, gate_logits, gp, gq, win)
-
-
-def body(queries, keys, values, gate_logits, sel_ids, pos_k, pos_v, mix_k, mix_v):
-    gp, gq, win = gather(keys, values, pos_k, pos_v, mix_k, mix_v)
-    return attend(sel_ids, queries, gate_logits, gp, gq, win)
+        compiler_params=pltpu.CompilerParams(
+            collective_id=0, has_side_effects=True, vmem_limit_bytes=VMEM_LIMIT
+        ),
+    )(sel_ids, *turned)
 
 
 def solution(mesh):

time: 99.7 us -> 79.9 us (0.80)
  local copies, waits for them, and re-layouts: 12.1 us -> 1.88 us
  Pallas kernels: 87.2 us -> 77.8 us
    unnamed x18 -> x1, local copies, waits for them, and re-layouts: 12.1 us -> 1.88 us
    pallas_call x2 -> x1, Pallas kernels: 87.2 us -> 77.8 us  [body(): pl.pallas_call(fused_kernel, out_shape=jax.ShapeDtypeStruct((TOKENS, HEAD...]
where the time goes in v2:
time: 79.9 us; the launch traced here: 79.7 us
  Pallas kernels  77.8 us (97%)
  local copies, waits for them, and re-layouts  1.88 us (2%)
    pallas_call x1, Pallas kernels, body(): pl.pallas_call(fused_kernel, out_shape=jax.ShapeDtypeStruct((TOKENS, HEAD...  77.8 us
    unnamed x1, local copies, waits for them, and re-layouts  1.88 us

profile of v2, /device:TPU:1, one launch (start us, length us, event | category | flops | bytes accessed | tf_op | source)
XLA Modules:
  0.0 79.7 jit_solution(4824318297675270468)
XLA Ops:
  0.0 77.8 %shard_map.91 = bf16[128,2048]{1,0:T(8,128)(2,1)} custom-call(s32[8,16]{1,0:T(8,128)} %sel.1, bf16[128,3072]{1,0:T(8,128)(2,1)} %q_in.1, bf16[2,192,128]{2,1,0:T(8,128)(2,1)} %bitcast.2, bf16[2,128,128]{2,1,0:T(8,128)(2,1)} %values_in.1, bf16[48,128]{1,0:T(8,128)(2,1)} %bitcast.3, bf16[32,192]{1,0:T(8,128)(2,1)} %pos_k_in.1, bf16[32,128]{1,0:T(8,128)(2,1)} %pos_v_in.1, ...), custom_call_target="tpu_custom_call" | custom-call | tf_op jit(solution)/shard_map/pallas_call | solution.py:360
  77.8 1.9 %copy.11 = bf16[128,2048]{1,0:T(8,128)(2,1)} copy(bf16[128,2048]{1,0:T(8,128)(2,1)} %shard_map.91) | data formatting | bytes 1048576

commit v3 on v2

--- a/solution.py
+++ b/solution.py
@@ -205,13 +205,13 @@
     for o in (0, 1, 2):
         ref = win.at[2 * o + 1 - c]
         remote(ref, other, wsend.at[0], wrecv.at[o if o == 0 else 2 + o]).wait_recv()
-    window_keys(win, kx, vx, bias, c)
+    window_keys(win, kx.at[0], vx.at[0], bias, c)
 
     def loop(k, carry):
         step(k, False)
-        window_heads(2 * (k - 3), qs, gate_rows, acc, kx, vx, bias)
+        for i in (0, 1):
+            window_heads(2 * (k - 3) + i, qs, gate_rows, acc, kx.at[0], vx.at[0], bias)
         lag1(k - 1)
-        window_heads(2 * (k - 3) + 1, qs, gate_rows, acc, kx, vx, bias)
         lag2(k - 2)
         return carry
 
@@ -234,7 +234,7 @@
     theirs = pl.ds((1 - c) * CHIPS, CHIPS)
     for n, buf in enumerate((gp, gq)):
         remote(buf.at[theirs], other, send.at[2 + n], d2d.at[n]).wait_recv()
-    compressed_part(gq, qs, gate_rows, acc, kx, vx, bias, me)
+    compressed_part(gq, qs, gate_rows, acc, kx.at[1], vx.at[1], bias, me)
     selected_part(sel, gp, gq, win, qs, gate_rows, acc, kx, vx, out, c)
     for n, buf in enumerate((gp, gq)):
         remote(buf.at[0 : CHIPS - 1], other, send.at[n], d2d.at[n]).wait_send()
@@ -263,7 +263,7 @@
     g = jax.nn.sigmoid(gates[...].astype(F32)).T
     for i in range(3 * HEADS):
         gate_rows[i] = jnp.broadcast_to(g[:, i : i + 1], (TOKENS, DV))
-    vx[:, 128:256] = jnp.ones((vx.shape[0], 128), BF)
+    vx[:, :, 128:256] = jnp.ones((2, vx.shape[1], 128), BF)
 
 
 def window_keys(win, kx, vx, bias, c):
@@ -312,14 +312,15 @@
         acc[at] += o * gate_rows[at]
         return carry
 
-    lax.fori_loop(0, HEADS // 2, heads, 0)
-
-
-def selected_part(sel, gp, gq, win, qs, gate_rows, acc, kx, vx, out, c):
+    lax.fori_loop(0, HEADS // 2, heads, 0, unroll=True)
+
+
+def selected_part(sel, gp, gq, win, qs, gate_rows, acc, key_slots, value_slots, out, c):
     count = TOPN * SEL_BLOCK
 
     def group(g, carry):
         mine = g // 4
+        kx, vx = key_slots.at[g % 2], value_slots.at[g % 2]
         kx[0:64, 0:128] = win[c, pl.ds(pl.multiple_of(mine * 64, 64), 64)]
         vx[0:64, 0:128] = win[c, pl.ds(pl.multiple_of(128 + mine * 64, 64), 64)]
         high = win[c, 256:320]
@@ -348,7 +349,7 @@
             out[rows, h * DV : (h + 1) * DV] = o[h].astype(BF)
         return carry
 
-    lax.fori_loop(0, QBLOCK // 2, group, 0)
+    lax.fori_loop(0, QBLOCK // 2, group, 0, unroll=True)
 
 
 def body(queries, keys, values, gate_logits, sel_ids, pos_k, pos_v, mix_k, mix_v):
@@ -371,8 +372,8 @@
             pltpu.VMEM((HEADS, TOKENS, 256), BF),
             pltpu.VMEM((3 * HEADS, TOKENS, DV), F32),
             pltpu.VMEM((HEADS, TOKENS, DV), F32),
-            pltpu.VMEM((1024, 256), BF),
-            pltpu.VMEM((1024, 256), BF),
+            pltpu.VMEM((2, 1024, 256), BF),
+            pltpu.VMEM((2, 1024, 256), BF),
             pltpu.VMEM((TOKENS, 1024), F32),
             dma((2, 9, 4)),
             dma((2, 9)),

time: 79.9 us -> 72.2 us (0.904)
  Pallas kernels: 77.8 us -> 70.1 us
    pallas_call x1, Pallas kernels: 77.8 us -> 70.1 us  [body(): pl.pallas_call(fused_kernel, out_shape=jax.ShapeDtypeStruct((TOKENS, HEAD...]
where the time goes in v3:
time: 72.2 us; the launch traced here: 72 us
  Pallas kernels  70.1 us (97%)
  local copies, waits for them, and re-layouts  1.88 us (3%)
    pallas_call x1, Pallas kernels, body(): pl.pallas_call(fused_kernel, out_shape=jax.ShapeDtypeStruct((TOKENS, HEAD...  70.1 us
    unnamed x1, local copies, waits for them, and re-layouts  1.88 us

profile of v3, /device:TPU:1, one launch (start us, length us, event | category | flops | bytes accessed | tf_op | source)
XLA Modules:
  0.0 72.0 jit_solution(327203100167654777)
XLA Ops:
  0.0 70.1 %shard_map.91 = bf16[128,2048]{1,0:T(8,128)(2,1)} custom-call(s32[8,16]{1,0:T(8,128)} %sel.1, bf16[128,3072]{1,0:T(8,128)(2,1)} %q_in.1, bf16[2,192,128]{2,1,0:T(8,128)(2,1)} %bitcast.2, bf16[2,128,128]{2,1,0:T(8,128)(2,1)} %values_in.1, bf16[48,128]{1,0:T(8,128)(2,1)} %bitcast.3, bf16[32,192]{1,0:T(8,128)(2,1)} %pos_k_in.1, bf16[32,128]{1,0:T(8,128)(2,1)} %pos_v_in.1, ...), custom_call_target="tpu_custom_call" | custom-call | tf_op jit(solution)/shard_map/pallas_call | solution.py:361
  70.1 1.9 %copy.11 = bf16[128,2048]{1,0:T(8,128)(2,1)} copy(bf16[128,2048]{1,0:T(8,128)(2,1)} %shard_map.91) | data formatting | bytes 1048576

commit v4 on v3

--- a/solution.py
+++ b/solution.py
@@ -67,6 +67,7 @@
     def chip_dev(offset):
         return (chip + offset + CHIPS) % CHIPS * 2 + c
 
+    across = dev(z, x + 2)
     near = [chip_dev(o) for o in (1, 2, -1, -2)]
     ins = (keys_in, values_in, pos_k_in, pos_v_in, mix_k_in, mix_v_in, gates_in, q_in)
     staged = (keys, values, pos_k, pos_v, mix_k, mix_v, gates, q)
@@ -74,82 +75,86 @@
     for cp in local:
         cp.start()
     bar = pltpu.get_barrier_semaphore()
-    for d in (*zn, *xn, other, *near):
+    for d in (*zn, *xn, across, other, *near):
         pl.semaphore_signal(bar, inc=1, device_id={"ctx": d}, device_id_type=MESH)
-    for cp in local[:6]:
+    me_s = slot(z, x)
+    local[0].wait()
+    row = keys[0].astype(F32).T.astype(BF)
+    gp[me_s] = row[:, 0:128]
+    pl.semaphore_wait(bar, 10)
+
+    def remote(ref, d, ss, rs, dst=None):
+        return pltpu.make_async_remote_copy(
+            src_ref=ref, dst_ref=ref if dst is None else dst, send_sem=ss, recv_sem=rs,
+            device_id={"ctx": d}, device_id_type=MESH,
+        )
+
+    def part(buf, s, rows):
+        return buf.at[s] if rows is None else buf.at[s, rows[0] : rows[1]]
+
+    def sp(s, rows, d, rs):
+        remote(part(gp, s, rows), d, send.at[0], rs).start()
+
+    def sq(s, rows, d, rs):
+        remote(part(gq, s, rows), d, send.at[1], rs).start()
+
+    def wp(s, rows, rs):
+        remote(part(gp, s, rows), other, send.at[0], rs).wait_recv()
+
+    def wq(s, rows, rs):
+        remote(part(gq, s, rows), other, send.at[1], rs).wait_recv()
+
+    def zsend_p(zz, r, d, k, half):
+        sp(slot(zz, x + r), P_HALF[d] if half else None, zn[d], pz.at[d, k, r])
+
+    def zsend_q(zz, d, k, half):
+        sq(slot(zz, x), Q_HALF[d] if half else None, zn[d], qz.at[d, k])
+
+    def xsend_q(zz, t, late=False):
+        if late:
+            sq(slot(zz, x), None, across, qx.at[t, 2])
+        for d in (0, 1):
+            sq(slot(zz, x), None, xn[d], qx.at[t, d])
+
+    def d2d_p(zz):
+        remote(gp.at[zrow(zz)], other, send.at[2], d2d.at[0]).start()
+
+    def d2d_q(zz):
+        remote(gq.at[zrow(zz)], other, send.at[3], d2d.at[1]).start()
+
+    sp(me_s, None, across, px.at[2])
+    for d in (0, 1):
+        sp(me_s, None, xn[d], px.at[d])
+    for d in (0, 1):
+        zsend_p(z, 0, d, 1, False)
+    for cp in local[1:6]:
         cp.wait()
-    me_s = slot(z, x)
-    rows = [keys[r].astype(F32).T.astype(BF) for r in (0, 1)]
-    for r in (0, 1):
-        span[r, 0:128] = rows[r][:, 0:128]
-        span[r, 128:256] = values[r]
-        span[r, 256:320] = paired_high(rows[r])
-    gp[me_s] = span[0, 0:128]
+    last_row = keys[1].astype(F32).T.astype(BF)
+    rows = (row, last_row)
     gq[me_s, VAL : VAL + 128] = values[0]
-    gq[me_s, HI : HI + 64] = span[0, 256:320]
+    gq[me_s, HI : HI + 64] = paired_high(row)
     ck = compressed(rows, pos_k[...], mix_k[...])
     cv = compressed(values, pos_v[...], mix_v[...])
     gq[me_s, CMP : CMP + 16] = jnp.concatenate([ck[:, 0:128], cv], axis=0).astype(BF)
     hi = jnp.concatenate([ck[:, 128:192], jnp.zeros((8, 64), F32)], axis=1)
     gq[me_s, CMP + 16 : CMP + 32] = jnp.concatenate([hi, jnp.zeros((8, 128), F32)], axis=0).astype(BF)
-    win[c] = span[1]
-    pl.semaphore_wait(bar, 9)
-
-    def remote(ref, d, ss, rs, dst=None):
-        return pltpu.make_async_remote_copy(
-            src_ref=ref, dst_ref=ref if dst is None else dst, send_sem=ss, recv_sem=rs,
-            device_id={"ctx": d}, device_id_type=MESH,
-        )
-
-    def part(buf, s, rows):
-        return buf.at[s] if rows is None else buf.at[s, rows[0] : rows[1]]
-
-    def sp(s, rows, d, rs):
-        remote(part(gp, s, rows), d, send.at[0], rs).start()
-
-    def sq(s, rows, d, rs):
-        remote(part(gq, s, rows), d, send.at[1], rs).start()
-
-    def wp(s, rows, rs):
-        remote(part(gp, s, rows), other, send.at[0], rs).wait_recv()
-
-    def wq(s, rows, rs):
-        remote(part(gq, s, rows), other, send.at[1], rs).wait_recv()
-
-    def zsend_p(zz, r, d, k, half):
-        sp(slot(zz, x + r), P_HALF[d] if half else None, zn[d], pz.at[d, k, r])
-
-    def zsend_q(zz, d, k, half):
-        sq(slot(zz, x), Q_HALF[d] if half else None, zn[d], qz.at[d, k])
-
-    def xsend_q(zz, t):
-        for d in (0, 1):
-            sq(slot(zz, x), None, xn[d], qx.at[t, d])
-
-    def d2d_p(zz):
-        remote(gp.at[zrow(zz)], other, send.at[2], d2d.at[0]).start()
-
-    def d2d_q(zz):
-        remote(gq.at[zrow(zz)], other, send.at[3], d2d.at[1]).start()
-
-    for d in (0, 1):
-        sp(me_s, None, xn[d], px.at[d])
     for d in (0, 1):
         zsend_q(z, d, 1, False)
-    for d in (0, 1):
-        zsend_p(z, 0, d, 1, False)
     xsend_q(z, 0)
+    for r in (0, 1):
+        span[r, 0:128] = rows[r][:, 0:128]
+        span[r, 128:256] = values[r]
+        span[r, 256:320] = paired_high(rows[r])
+    win[c] = span[1]
     for o in (1, 2):
         wrapped = jnp.where(chip + o >= CHIPS, 0, 1)
         remote(span.at[wrapped], near[o - 1], wsend.at[o], wrecv.at[o], win.at[2 * o + c]).start()
     remote(win.at[c], other, wsend.at[0], wrecv.at[0]).start()
     for d, r in ((0, 3), (1, 1)):
         wp(slot(z, x + r), None, px.at[d])
-        sp(slot(z, x + r), P_HALF[d], xn[d], px.at[2 + d])
         for e in (0, 1):
             zsend_p(z, r, e, 1, False)
-    for d in (0, 1):
-        wp(slot(z, x + 2), P_HALF[d], px.at[2 + d])
+    wp(slot(z, x + 2), None, px.at[2])
     for e in (0, 1):
         zsend_p(z, 2, e, 1, False)
     d2d_p(z)
@@ -157,13 +162,17 @@
         cp.wait()
     prepare(q, gates, qs, gate_rows, vx)
 
-    def qx_full(zz, t):
+    def qx_full(zz, t, late=False):
         for d, r in ((0, 3), (1, 1)):
             wq(slot(zz, x + r), None, qx.at[t, d])
+            if late:
+                continue
             sq(slot(zz, x + r), Q_HALF[d], xn[d], qx.at[t, 2 + d])
 
-    def qx_half(zz, t):
-        for d in (0, 1):
+    def qx_half(zz, t, late=False):
+        if late:
+            wq(slot(zz, x + 2), None, qx.at[t, 2])
+        for d in () if late else (0, 1):
             wq(slot(zz, x + 2), Q_HALF[d], qx.at[t, 2 + d])
         d2d_q(zz)
 
@@ -221,16 +230,16 @@
     lag2(5)
     for d in (0, 1):
         wq(slot(z - 8, x), Q_HALF[d], qz.at[d, 8])
-    xsend_q(z - 8, 8)
+    xsend_q(z - 8, 8, True)
     for r in (0, 3, 1, 2):
         for d in (0, 1):
             wp(slot(z - 8, x + r), P_HALF[d], pz.at[d, 8, r])
     d2d_p(z - 8)
     lag1(7)
     lag2(6)
-    qx_full(z - 8, 8)
+    qx_full(z - 8, 8, True)
     lag2(7)
-    qx_half(z - 8, 8)
+    qx_half(z - 8, 8, True)
     theirs = pl.ds((1 - c) * CHIPS, CHIPS)
     for n, buf in enumerate((gp, gq)):
         remote(buf.at[theirs], other, send.at[2 + n], d2d.at[n]).wait_recv()

time: 72.2 us -> 70.2 us (0.972)
  Pallas kernels: 70.1 us -> 68.1 us
    pallas_call x1, Pallas kernels: 70.1 us -> 68.1 us  [body(): pl.pallas_call(fused_kernel, out_shape=jax.ShapeDtypeStruct((TOKENS, HEAD...]
where the time goes in v4:
time: 70.2 us; the launch traced here: 70 us
  Pallas kernels  68.1 us (97%)
  local copies, waits for them, and re-layouts  1.88 us (3%)
    pallas_call x1, Pallas kernels, body(): pl.pallas_call(fused_kernel, out_shape=jax.ShapeDtypeStruct((TOKENS, HEAD...  68.1 us
    unnamed x1, local copies, waits for them, and re-layouts  1.88 us

profile of v4, /device:TPU:1, one launch (start us, length us, event | category | flops | bytes accessed | tf_op | source)
XLA Modules:
  0.0 70.0 jit_solution(1865861934579426554)
XLA Ops:
  0.0 68.1 %shard_map.91 = bf16[128,2048]{1,0:T(8,128)(2,1)} custom-call(s32[8,16]{1,0:T(8,128)} %sel.1, bf16[128,3072]{1,0:T(8,128)(2,1)} %q_in.1, bf16[2,192,128]{2,1,0:T(8,128)(2,1)} %bitcast.2, bf16[2,128,128]{2,1,0:T(8,128)(2,1)} %values_in.1, bf16[48,128]{1,0:T(8,128)(2,1)} %bitcast.3, bf16[32,192]{1,0:T(8,128)(2,1)} %pos_k_in.1, bf16[32,128]{1,0:T(8,128)(2,1)} %pos_v_in.1, ...), custom_call_target="tpu_custom_call" | custom-call | tf_op jit(solution)/shard_map/pallas_call | solution.py:370
  68.2 1.9 %copy.11 = bf16[128,2048]{1,0:T(8,128)(2,1)} copy(bf16[128,2048]{1,0:T(8,128)(2,1)} %shard_map.91) | data formatting | bytes 1048576

commit v5 on v4

--- a/solution.py
+++ b/solution.py
@@ -182,18 +182,26 @@
     def at_t(d, k):
         return k if d == 0 else 8 + k
 
-    def step(k, last):
+    def step(k, last, between=()):
         for d in (0, 1):
             wq(slot(at_z(d, k), x), None, qz.at[d, k])
             zsend_q(at_z(d, k), d, k + 1, last)
             xsend_q(at_z(d, k), at_t(d, k))
-        for r in (0, 3, 1, 2):
+        for n, r in enumerate((0, 3, 1, 2)):
             for d in (0, 1):
                 wp(slot(at_z(d, k), x + r), None, pz.at[d, k, r])
                 zsend_p(at_z(d, k), r, d, k + 1, last)
+            if n < len(between):
+                between[n]()
         for d in (0, 1):
             d2d_p(at_z(d, k))
 
+    def full(d, k):
+        return lambda: qx_full(at_z(d, k), at_t(d, k))
+
+    def half(d, k):
+        return lambda: qx_half(at_z(d, k), at_t(d, k))
+
     def lag1(k):
         for d in (0, 1):
             qx_full(at_z(d, k), at_t(d, k))
@@ -202,10 +210,8 @@
         for d in (0, 1):
             qx_half(at_z(d, k), at_t(d, k))
 
-    step(1, False)
-    qx_full(z, 0)
-    step(2, False)
-    lag1(1)
+    step(1, False, (lambda: qx_full(z, 0),))
+    step(2, False, (full(0, 1), full(1, 1)))
     qx_half(z, 0)
     for o in (1, 2):
         remote(win.at[2 * o + c], other, wsend.at[o], wrecv.at[o]).wait_recv()
@@ -217,26 +223,24 @@
     window_keys(win, kx.at[0], vx.at[0], bias, c)
 
     def loop(k, carry):
-        step(k, False)
+        step(k, False, (full(0, k - 1), full(1, k - 1)))
         for i in (0, 1):
             window_heads(2 * (k - 3) + i, qs, gate_rows, acc, kx.at[0], vx.at[0], bias)
-        lag1(k - 1)
         lag2(k - 2)
         return carry
 
     lax.fori_loop(3, 7, loop, 0)
-    step(7, True)
-    lag1(6)
+    step(7, True, (full(0, 6), full(1, 6)))
     lag2(5)
     for d in (0, 1):
         wq(slot(z - 8, x), Q_HALF[d], qz.at[d, 8])
     xsend_q(z - 8, 8, True)
-    for r in (0, 3, 1, 2):
+    late = (full(0, 7), full(1, 7), half(0, 6), half(1, 6))
+    for n, r in enumerate((0, 3, 1, 2)):
         for d in (0, 1):
             wp(slot(z - 8, x + r), P_HALF[d], pz.at[d, 8, r])
+        late[n]()
     d2d_p(z - 8)
-    lag1(7)
-    lag2(6)
     qx_full(z - 8, 8, True)
     lag2(7)
     qx_half(z - 8, 8, True)

time: 70.2 us -> 69.1 us (0.984)
  Pallas kernels: 68.1 us -> 67 us
    pallas_call x1, Pallas kernels: 68.1 us -> 67 us  [body(): pl.pallas_call(fused_kernel, out_shape=jax.ShapeDtypeStruct((TOKENS, HEAD...]
where the time goes in v5:
time: 69.1 us; the launch traced here: 68.9 us
  Pallas kernels  67 us (97%)
  local copies, waits for them, and re-layouts  1.88 us (3%)
    pallas_call x1, Pallas kernels, body(): pl.pallas_call(fused_kernel, out_shape=jax.ShapeDtypeStruct((TOKENS, HEAD...  67 us
    unnamed x1, local copies, waits for them, and re-layouts  1.88 us

profile of v5, /device:TPU:1, one launch (start us, length us, event | category | flops | bytes accessed | tf_op | source)
XLA Modules:
  0.0 68.9 jit_solution(6855475751295883600)
XLA Ops:
  0.0 67.0 %shard_map.91 = bf16[128,2048]{1,0:T(8,128)(2,1)} custom-call(s32[8,16]{1,0:T(8,128)} %sel.1, bf16[128,3072]{1,0:T(8,128)(2,1)} %q_in.1, bf16[2,192,128]{2,1,0:T(8,128)(2,1)} %bitcast.2, bf16[2,128,128]{2,1,0:T(8,128)(2,1)} %values_in.1, bf16[48,128]{1,0:T(8,128)(2,1)} %bitcast.3, bf16[32,192]{1,0:T(8,128)(2,1)} %pos_k_in.1, bf16[32,128]{1,0:T(8,128)(2,1)} %pos_v_in.1, ...), custom_call_target="tpu_custom_call" | custom-call | tf_op jit(solution)/shard_map/pallas_call | solution.py:374
  67.0 1.9 %copy.11 = bf16[128,2048]{1,0:T(8,128)(2,1)} copy(bf16[128,2048]{1,0:T(8,128)(2,1)} %shard_map.91) | data formatting | bytes 1048576

commit v6 on v5

--- a/solution.py
+++ b/solution.py
@@ -245,9 +245,9 @@
     lag2(7)
     qx_half(z - 8, 8, True)
     theirs = pl.ds((1 - c) * CHIPS, CHIPS)
-    for n, buf in enumerate((gp, gq)):
-        remote(buf.at[theirs], other, send.at[2 + n], d2d.at[n]).wait_recv()
+    remote(gq.at[theirs], other, send.at[3], d2d.at[1]).wait_recv()
     compressed_part(gq, qs, gate_rows, acc, kx.at[1], vx.at[1], bias, me)
+    remote(gp.at[theirs], other, send.at[2], d2d.at[0]).wait_recv()
     selected_part(sel, gp, gq, win, qs, gate_rows, acc, kx, vx, out, c)
     for n, buf in enumerate((gp, gq)):
         remote(buf.at[0 : CHIPS - 1], other, send.at[n], d2d.at[n]).wait_send()

time: 69.1 us -> 69.5 us (level)
  no operation moved by 1% of the time
where the time goes in v6:
time: 69.5 us; the launch traced here: 69.3 us
  Pallas kernels  67.4 us (97%)
  local copies, waits for them, and re-layouts  1.88 us (3%)
    pallas_call x1, Pallas kernels, body(): pl.pallas_call(fused_kernel, out_shape=jax.ShapeDtypeStruct((TOKENS, HEAD...  67.4 us
    unnamed x1, local copies, waits for them, and re-layouts  1.88 us

profile of v6, /device:TPU:1, one launch (start us, length us, event | category | flops | bytes accessed | tf_op | source)
XLA Modules:
  0.0 69.3 jit_solution(17575817425118827438)
XLA Ops:
  0.0 67.4 %shard_map.91 = bf16[128,2048]{1,0:T(8,128)(2,1)} custom-call(s32[8,16]{1,0:T(8,128)} %sel.1, bf16[128,3072]{1,0:T(8,128)(2,1)} %q_in.1, bf16[2,192,128]{2,1,0:T(8,128)(2,1)} %bitcast.2, bf16[2,128,128]{2,1,0:T(8,128)(2,1)} %values_in.1, bf16[48,128]{1,0:T(8,128)(2,1)} %bitcast.3, bf16[32,192]{1,0:T(8,128)(2,1)} %pos_k_in.1, bf16[32,128]{1,0:T(8,128)(2,1)} %pos_v_in.1, ...), custom_call_target="tpu_custom_call" | custom-call | tf_op jit(solution)/shard_map/pallas_call | solution.py:374
  67.4 1.9 %copy.11 = bf16[128,2048]{1,0:T(8,128)(2,1)} copy(bf16[128,2048]{1,0:T(8,128)(2,1)} %shard_map.91) | data formatting | bytes 1048576
